TPU v7x, 512 devices: a whole 4x4x16 slice. The times are simulated.
512 devices in a mesh: pair: 128 (over y, z, core), red: 4 (over x).
Axes of the slice: x: 4, y: 4, z: 16, core: 2. Of those that a mesh axis runs over, the one named last changes fastest.
Arguments:
- amplitudes: bfloat16 [2048, 4096], P('pair', 'red'), may hold values from -6 to 6
- integrals: bfloat16 [4096, 65536], P('red', 'pair'), may hold values from -0.125 to 0.125
- pattern: int32 [128, 64], P('pair', 'red'), may hold values from 0 to 1, as said below
Outputs:
- ladder_term: bfloat16 [128, 16, 65536], P(None, 'red', 'pair')
Inputs may be any that keep to these rules, and one draw needn't show every extreme that they name: `pattern`: in every tile, exactly 8 of each aligned group of 16 blocks are 1.
All inputs are finite; a program needn't handle non-finite values.
Results may differ from a plain program's by a relative error of at most 0.0013.
Values may be sent and summed in bfloat16 or wider, within the bound.
A program may use at most 64 MiB of HBM per device.

v0:
```python
import jax
import jax.numpy as jnp
from jax import lax
from jax.sharding import PartitionSpec as P


def shards(amplitudes, integrals, pattern):
    tile_rows = amplitudes.shape[0]
    blocks = pattern.shape[1]
    block_width = amplitudes.shape[1] // blocks
    out_width = integrals.shape[1]
    keep_mask = jnp.repeat(jnp.repeat(pattern, tile_rows, axis=0), block_width, axis=1).astype(
        jnp.bfloat16
    )
    masked = amplitudes * keep_mask
    partial_value = jnp.dot(
        lax.all_gather(masked, "pair", axis=0, tiled=True),
        integrals,
        preferred_element_type=jnp.float32,
    )
    tile_count = partial_value.shape[0] // tile_rows
    summed = lax.psum_scatter(
        partial_value.reshape(tile_count, tile_rows, out_width),
        "red",
        scatter_dimension=1,
        tiled=True,
    )
    return summed.astype(jnp.bfloat16)


def solution(mesh):
    placed = (P("pair", "red"), P("red", "pair"), P("pair", "red"))
    return jax.shard_map(
        shards, mesh=mesh, in_specs=placed, out_specs=P(None, "red", "pair"), check_vma=False
    )
```

profile of v0, /device:TPU:1, one launch (start us, length us, event | category | flops | bytes accessed | tf_op | source)
XLA Modules:
  0.0 226.7 jit_solution(17842721416136384331)
XLA Ops:
  6.5 0.0 copy-start
  6.5 0.0 all-gather.2.cloned.1.call-start
  6.5 0.7 convert_bitcast_fusion
  7.3 0.1 broadcast_in_dim.6
  7.4 0.1 convert_element_type.16
  7.4 1.4 broadcast_multiply_fusion
  8.8 0.0 all-gather.2.cloned.1.call-update
  8.9 0.0 reduce-scatter.2.cloned.1.call-start
  8.9 149.4 %all-gather.2.cloned.1.call-done = bf16[2048,1024]{1,0:T(8,128)(2,1)} async-done(((bf16[16,1024]{1,0:T(8,128)(2,1)}), bf16[2048,1024]{1,0:T(8,128)(2,1)}) %all-gather.2.cloned.1.call-update) | async-done | bytes 4194320 | tf_op jit(solution)/shard_map/all_gather | solution.py:17
  158.3 0.0 copy-done
  158.3 4.5 %fusion = f32[2048,512]{1,0:T(8,128)S(1)} fusion(bf16[2048,1024]{1,0:T(8,128)(2,1)} %all-gather.2.cloned.1.call-done, bf16[1024,512]{1,0:T(8,128)(2,1)S(1)} %copy-done), kind=kOutput, calls=%fused_computation.2 | convolution fusion | flops 2147483648 | bytes 9437184 | tf_op jit(solution)/shard_map/dot_general | solution.py:16
  162.8 4.4 %copy.4 = f32[128,16,512]{2,0,1:T(8,128)} copy(f32[128,16,512]{2,1,0:T(8,128)S(1)} %bitcast.5) | data formatting | bytes 8388608 | tf_op jit(solution)/shard_map/reshape | solution.py:23
  167.2 0.0 reduce-scatter.2.cloned.1.call-update
  167.2 50.2 %reduce-scatter.2.cloned.1.call-done = f32[128,4,512]{2,0,1:T(8,128)} async-done(((f32[128,16,512]{2,0,1:T(8,128)}), f32[128,4,512]{2,0,1:T(8,128)}) %reduce-scatter.2.cloned.1.call-update) | async-done | bytes 1048592 | tf_op jit(solution)/shard_map/reduce_scatter | solution.py:22
  217.3 1.3 convert_element_type.17
  218.6 1.2 copy.5
Async XLA Ops:
  6.5 151.7 %copy-start = (bf16[1024,512]{1,0:T(8,128)(2,1)S(1)}, bf16[1024,512]{1,0:T(8,128)(2,1)}, u32[]{:S(2)}) copy-start(bf16[1024,512]{1,0:T(8,128)(2,1)} %param.4) | copy-start | bytes 3145732
  6.5 151.7 %all-gather.2.cloned.1.call-start = ((), (), s32[]{:S(2)}) async-start(), calls=%async_computation.1 | async-start | bytes 4227072 | tf_op jit(solution)/shard_map/all_gather | solution.py:17
  8.9 208.5 %reduce-scatter.2.cloned.1.call-start = ((), (), s32[]{:S(2)}) async-start(), calls=%async_computation.2 | async-start | bytes 5242880 | tf_op jit(solution)/shard_map/reduce_scatter | solution.py:22
Sparse Core Ops, SparseCore 0:
  10.5 147.7 all-gather.1
  167.3 49.9 reduce-scatter.1
where the time goes:
time: 227 us
  waiting for transfers between devices  200 us (88%)
  between operations  13.4 us (6%)
  local copies, waits for them, and re-layouts  5.73 us (3%)
  matrix products  4.53 us (2%)
  other arithmetic  3.41 us (2%)
    all_gather x1, waiting for transfers between devices, shards(): lax.all_gather(masked, 'pair', axis=0, tiled=True)  149 us
    reduce_scatter x1, waiting for transfers between devices, shards(): lax.psum_scatter(partial_value.reshape(tile_count, tile_rows, out_width),...  50.2 us
  transfers between devices with their start and end apart: 2, of which 2 were waited for; matrix products, arithmetic and copies ran while one was open for 0% of the time, Pallas kernels for 0%

commit v1 on v0

--- a/solution.py
+++ b/solution.py
@@ -14,7 +14,9 @@
     )
     masked = amplitudes * keep_mask
     partial_value = jnp.dot(
-        lax.all_gather(masked, "pair", axis=0, tiled=True),
+        jnp.concatenate(
+            lax.all_to_all(jnp.stack([masked] * lax.axis_size("pair")), "pair", 0, 0), axis=0
+        ),
         integrals,
         preferred_element_type=jnp.float32,
     )

time: 227 us -> 283 us (1.25)
  blocking collectives: 0 us -> 206 us
  waiting for transfers between devices: 200 us -> 51.5 us
  local copies, waits for them, and re-layouts: 5.73 us -> 1.89 us
    all_to_all x0 -> x1, blocking collectives: none -> 206 us  [shards(): lax.all_to_all(jnp.stack([masked] * lax.axis_size('pair')), 'pair', 0, 0)]
    all_gather x1 -> x0, waiting for transfers between devices: 149 us -> none  [shards(): lax.all_gather(masked, 'pair', axis=0, tiled=True)]
    reshape x1 -> x0, local copies, waits for them, and re-layouts: 4.37 us -> none  [shards(): partial_value.reshape(tile_count, tile_rows, out_width)]
  transfers between devices with their start and end apart: 2 -> 1, of which waited for: 2 -> 1; matrix products, arithmetic and copies ran while one was open for 0% -> 0% of each run, Pallas kernels for 0% -> 0%
where the time goes in v1:
time: 283 us
  blocking collectives  206 us (73%)
  waiting for transfers between devices  51.5 us (18%)
  between operations  13.4 us (5%)
  matrix products  7.01 us (2%)
    all_to_all x1, blocking collectives, shards(): lax.all_to_all(jnp.stack([masked] * lax.axis_size('pair')), 'pair', 0, 0)  206 us
    reduce_scatter x1, waiting for transfers between devices, shards(): lax.psum_scatter(partial_value.reshape(tile_count, tile_rows, out_width),...  51.5 us
    dot_general x1, matrix products, shards(): jnp.dot(jnp.concatenate(lax.all_to_all(jnp.stack([masked] * lax.axis_size...  7.01 us
  transfers between devices with their start and end apart: 1, of which 1 were waited for; matrix products, arithmetic and copies ran while one was open for 0% of the time, Pallas kernels for 0%

profile of v1, /device:TPU:1, one launch (start us, length us, event | category | flops | bytes accessed | tf_op | source)
XLA Modules:
  0.0 282.6 jit_solution(10264506776064788397)
XLA Ops:
  6.5 0.0 copy-start
  6.5 0.0 reduce-scatter.2.cloned.1.call-start
  6.5 0.7 convert_bitcast_fusion
  7.3 0.1 broadcast_in_dim.6
  7.4 0.1 convert_element_type.16
  7.4 0.8 broadcast_multiply_fusion
  8.2 0.5 stack.2
  8.7 206.0 %all_to_all.5 = bf16[128,16,1024]{2,1,0:T(8,128)(2,1)S(1)} all-to-all(bf16[128,16,1024]{2,1,0:T(8,128)(2,1)S(1)} %stack.2), channel_id=1, replica_groups=mesh['pair'=128,'red'=4] {'pair'}, dimensions={0} | all-to-all | bytes 8388608 | tf_op jit(solution)/shard_map/all_to_all | solution.py:18
  214.7 0.0 copy-done
  214.7 7.0 %fusion = f32[128,16,512]{2,0,1:T(8,128)} fusion(bf16[128,16,1024]{2,1,0:T(8,128)(2,1)S(1)} %all_to_all.5, bf16[1024,512]{1,0:T(8,128)(2,1)S(1)} %copy-done), kind=kOutput, calls=%fused_computation | convolution fusion | flops 2147483648 | bytes 9437184 | tf_op jit(solution)/shard_map/dot_general | solution.py:16
  221.7 0.0 reduce-scatter.2.cloned.1.call-update
  221.8 51.5 %reduce-scatter.2.cloned.1.call-done = f32[128,4,512]{2,0,1:T(8,128)} async-done(((f32[128,16,512]{2,0,1:T(8,128)}), f32[128,4,512]{2,0,1:T(8,128)}) %reduce-scatter.2.cloned.1.call-update) | async-done | bytes 1048592 | tf_op jit(solution)/shard_map/reduce_scatter | solution.py:24
  273.3 1.3 convert_element_type.17
  274.6 1.2 copy.6
Async XLA Ops:
  6.5 208.2 %copy-start = (bf16[1024,512]{1,0:T(8,128)(2,1)S(1)}, bf16[1024,512]{1,0:T(8,128)(2,1)}, u32[]{:S(2)}) copy-start(bf16[1024,512]{1,0:T(8,128)(2,1)} %param.4) | copy-start | bytes 3145732
  6.5 266.8 %reduce-scatter.2.cloned.1.call-start = ((), (), s32[]{:S(2)}) async-start(), calls=%async_computation.2 | async-start | bytes 5242880 | tf_op jit(solution)/shard_map/reduce_scatter | solution.py:24
Sparse Core Ops, SparseCore 0:
  221.9 51.3 reduce-scatter.1
